TPU v7x, 32 devices: a whole 2x2x4 slice. The times are simulated.
32 devices in a mesh: groups: 2 (over y), blocks: 4 (over z), tiles: 2 (over x), sub: 2 (over core).
Axes of the slice: x: 2, y: 2, z: 4, core: 2. Of those that a mesh axis runs over, the one named last changes fastest.
Arguments:
- seg_feat: bfloat16 [8, 4, 2048, 128], P(('groups', 'tiles', 'sub'), 'blocks'), parts along dimension 0, may hold values from -6 to 6
- seg_block: int32 [8, 4, 2048, 1], P(('groups', 'tiles', 'sub'), 'blocks'), parts along dimension 0, may hold values from 0 to 3; in each aligned block of 2048 rows (0 to 2047, 2048 to 4095, ..., all dimensions but the last counted through in order) at most 1024 rows name the same one
- depth_rank: int32 [8, 4, 8, 256], P(('groups', 'tiles', 'sub'), 'blocks'), parts along dimension 0, may hold values from 0 to 7, as said below
- w_in: bfloat16 [4, 128, 512], P('blocks'), may hold values from -0.5 to 0.5
- w_hidden: bfloat16 [4, 4, 512, 512], P('blocks'), may hold values from -0.25 to 0.25
- w_out: bfloat16 [4, 512, 128], P('blocks'), may hold values from -0.25 to 0.25
- w_dens: bfloat16 [4, 512], P('blocks'), may hold values from -0.25 to 0.25
- conv_w: bfloat16 [3, 3, 3, 128, 128], replicated, may hold values from -0.1875 to 0.1875
Outputs:
- decoded: bfloat16 [128, 64, 128], P(('groups', 'tiles', 'sub'), 'blocks'), parts along dimension 0
There are 2 independent parts, one for each index of `groups`. A program takes and returns all parts, laid end to end along the dimension named above; an argument that names none is the same for every part. Nothing has to cross between parts.
Inputs may be any that keep to these rules, and one draw needn't show every extreme that they name: `seg_block`: among one device's 2048 segments, no block is named more than 1024 times; some device names some block exactly 1024 times. `depth_rank`: for every ray, its 8 segments' ranks are a permutation of 0 .. 7.
All inputs are finite; a program needn't handle non-finite values.
Results may differ from a plain program's by a relative error of at most 0.02.
Values may be sent and summed in bfloat16 or wider, within the bound.
A program may use at most 64 MiB of HBM per device.

v0:
```python
import functools

import jax
import jax.numpy as jnp
from jax import lax
from jax.experimental import pallas as pl
from jax.experimental.pallas import tpu as pltpu
from jax.sharding import PartitionSpec as P

SEGS_RAY = 8
CONV_LAYERS = 3
TW = 16
TH = 16
RAYS_DEV = 256
MESH = pl.DeviceIdType.MESH
F32 = jnp.float32
BF16 = jnp.bfloat16


def silu(value):
    half = value * jnp.asarray(0.5, value.dtype)
    return half + half * jnp.tanh(half)


def softplus(value):
    return jnp.maximum(value, 0.0) + jnp.log1p(jnp.exp(-jnp.abs(value)))


def block_at(step, place, count):
    near = jnp.minimum(place, count - 1 - place)
    distance = (step + 1) // 2
    paired = jnp.where(step % 2 == 1, place + distance, place - distance)
    rest = jnp.where(2 * place <= count - 1, step, count - 1 - step)
    return jnp.where(step <= 2 * near, paired, rest)


AROUND = [(dy, dx) for dy in (-1, 0, 1) for dx in (-1, 0, 1) if (dy, dx) != (0, 0)]
Z, X, Y, D, SA, SX, SY, SD, ZD = range(9)


def render_kernel(
    count,
    tiles_count,
    capacity,
    row_tile,
    feat_ref,
    block_ref,
    rank_ref,
    w_in_ref,
    w_hid_ref,
    w_out_ref,
    w_dens_ref,
    color_ref,
    hid,
    ends,
    slot_row,
    wide,
    turns,
    rays,
    act,
    heads,
    dens_map,
    around,
    edge_send,
    edge_recv,
    send_sem,
    recv_sem,
    ends_send,
    ends_recv,
    own_sem,
):
    place = lax.axis_index("blocks")
    tile = lax.axis_index("tiles")
    group = lax.axis_index("groups")
    core = lax.axis_index("sub")
    tile_mate = tile + 1 - 2 * (tile % 2)
    group_mate = group + 1 - 2 * (group % 2)
    core_mate = 1 - core
    tx, gy = tile % 2, group % 2
    layers = w_hid_ref.shape[0]
    hidden = w_hid_ref.shape[2]
    part = hidden // 8
    end_rows = ends.shape[1]
    end_half = end_rows // 2
    feats = w_out_ref.shape[1]
    in_width = w_in_ref.shape[0]
    segments = feat_ref.shape[0]

    def eighth(a, b, c):
        return (a * 2 + b) * 2 + c

    to_x, to_y, to_c = {"tiles": tile_mate}, {"groups": group_mate}, {"sub": core_mate}

    line = tile * 2 + core
    lines = 2 * tiles_count

    def beside(dy, dx):
        row, column = line + dy, place + dx
        exists = 1
        if dy < 0:
            exists = exists * jnp.minimum(line, 1)
        if dy > 0:
            exists = exists * jnp.minimum(lines - 1 - line, 1)
        if dx < 0:
            exists = exists * jnp.minimum(place, 1)
        if dx > 0:
            exists = exists * jnp.minimum(count - 1 - place, 1)
        return {"tiles": (row + 2) // 2 - 1, "sub": (row + 2) % 2, "blocks": column}, exists

    barrier = pltpu.get_barrier_semaphore()
    pl.semaphore_signal(barrier, inc=1, device_id=to_x, device_id_type=MESH)
    pl.semaphore_signal(barrier, inc=1, device_id=to_y, device_id_type=MESH)
    pl.semaphore_signal(barrier, inc=1, device_id=to_c, device_id_type=MESH)

    @pl.when(place > 0)
    def _():
        pl.semaphore_signal(barrier, inc=1, device_id={"blocks": place - 1}, device_id_type=MESH)

    @pl.when(place < count - 1)
    def _():
        pl.semaphore_signal(barrier, inc=1, device_id={"blocks": place + 1}, device_id_type=MESH)

    around[...] = jnp.zeros_like(around)
    own = pltpu.make_async_copy(w_hid_ref, hid.at[place], own_sem)
    own.start()
    ends[place, 0:in_width] = w_in_ref[...]
    ends[place, in_width : in_width + feats] = w_out_ref[...].T
    ends[place, in_width + feats : end_rows] = jnp.broadcast_to(
        w_dens_ref[...], (end_rows - in_width - feats, hidden)
    )
    own.wait()

    peers = 3 + jnp.minimum(place, 1) + jnp.minimum(count - 1 - place, 1)
    for dy, dx in AROUND:
        there, exists = beside(dy, dx)

        @pl.when(exists == 1)
        def _():
            pl.semaphore_signal(barrier, inc=1, device_id=there, device_id_type=MESH)

        peers = peers + exists
    pl.semaphore_wait(barrier, peers)

    def piece(block, layer, which):
        return hid.at[block, layer, pl.ds(pl.multiple_of(which * part, part), part)]

    def move(block, layer, which, kind, target, send_kind=None):
        ref = piece(block, layer, which)
        return pltpu.make_async_remote_copy(
            src_ref=ref,
            dst_ref=ref,
            send_sem=send_sem.at[block, layer, kind if send_kind is None else send_kind],
            recv_sem=recv_sem.at[block, layer, kind],
            device_id=target,
            device_id_type=MESH,
        )

    def move_ends(block, half, kind, target, send_kind=None):
        ref = ends.at[block, pl.ds(pl.multiple_of(half * end_half, end_half), end_half)]
        return pltpu.make_async_remote_copy(
            src_ref=ref,
            dst_ref=ref,
            send_sem=ends_send.at[block, kind if send_kind is None else send_kind],
            recv_sem=ends_recv.at[block, kind],
            device_id=target,
            device_id_type=MESH,
        )

    e_own = eighth(tx, gy, core)
    e_x = eighth(1 - tx, gy, core)
    e_y = eighth(tx, 1 - gy, core)
    e_d = eighth(1 - tx, 1 - gy, core)
    m_own = eighth(tx, gy, core_mate)
    m_x = eighth(1 - tx, gy, core_mate)
    m_y = eighth(tx, 1 - gy, core_mate)
    m_d = eighth(1 - tx, 1 - gy, core_mate)
    up, down = {"blocks": place + 1}, {"blocks": place - 1}

    def own_up(action):
        @pl.when(place < count - 1)
        def _():
            action(move_ends(place, core, 0, up))
            for layer in range(layers):
                action(move(place, layer, e_own, Z, up))

    def own_down(action):
        @pl.when(place > 0)
        def _():
            action(move_ends(place, core, 0, down, 2))
            for layer in range(layers):
                action(move(place, layer, e_own, Z, down, ZD))

    own_up(lambda c: c.start())
    own_down(lambda c: c.start())

    def onward(block, action):
        @pl.when((block < place) & (place < count - 1))
        def _():
            action(up)

        @pl.when((block > place) & (place > 0))
        def _():
            action(down)

    def arrive(block, layer):
        move(block, layer, e_own, Z, up).wait_recv()
        onward(block, lambda to: move(block, layer, e_own, Z, to).start())
        move(block, layer, e_own, X, to_x).start()
        move(block, layer, e_own, Y, to_y).start()
        move(block, layer, e_own, SA, to_c).start()

    def arrive_ends(block):
        move_ends(block, core, 0, up).wait_recv()
        onward(block, lambda to: move_ends(block, core, 0, to).start())
        move_ends(block, core, 1, to_c).start()

    def cross(block, layer):
        move(block, layer, e_x, X, to_x).wait_recv()
        move(block, layer, e_y, Y, to_y).wait_recv()

        @pl.when(core == 0)
        def _():
            move(block, layer, e_x, D, to_y).start()

        @pl.when(core == 1)
        def _():
            move(block, layer, e_y, D, to_x).start()

        move(block, layer, e_x, SX, to_c).start()
        move(block, layer, e_y, SY, to_c).start()

    def corner(block, layer):
        move(block, layer, e_d, D, to_x).wait_recv()
        move(block, layer, e_d, SD, to_c).start()

    def ready(block, layer):
        move(block, layer, m_own, SA, to_c).wait_recv()
        move(block, layer, m_x, SX, to_c).wait_recv()
        move(block, layer, m_y, SY, to_c).wait_recv()
        move(block, layer, m_d, SD, to_c).wait_recv()

    def item(step, layer, ahead):
        return step + (layer + ahead) // layers, (layer + ahead) % layers

    def exchange(step, layer):
        for ahead, action in ((4, arrive), (3, cross), (2, corner)):
            later, its_layer = item(step, layer, ahead)

            @pl.when((later > 0) & (later < count))
            def _():
                block = block_at(later, place, count)
                if action is arrive and its_layer == 0:
                    arrive_ends(block)
                action(block, its_layer)

    rows16 = 16
    chunks = segments // 128
    lane = lax.broadcasted_iota(jnp.int32, (128, 128), 1)
    sub = lax.broadcasted_iota(jnp.int32, (128, 128), 0)
    earlier = (sub < lane).astype(F32).astype(BF16)
    names = lax.broadcasted_iota(jnp.int32, (rows16, 128), 0)
    base = names.astype(F32) * capacity
    named = [
        (jnp.broadcast_to(block_ref[:, c * 128 : (c + 1) * 128], (rows16, 128)) == names).astype(F32)
        for c in range(chunks)
    ]
    before = jnp.dot(
        jnp.concatenate(named, axis=0).astype(BF16), earlier, preferred_element_type=F32
    )
    carry = base
    for c in range(chunks):
        ahead_of = before[c * rows16 : (c + 1) * rows16] + carry
        carry = carry + jnp.sum(named[c], axis=1, keepdims=True)
        slot_row[:, c * 128 : (c + 1) * 128] = jnp.sum(named[c] * ahead_of, axis=0, keepdims=True)
    wide[:, 0:in_width] = feat_ref[...]
    ray_of = lax.broadcasted_iota(jnp.int32, (RAYS_DEV, 128), 0)
    lane_of = lax.broadcasted_iota(jnp.int32, (RAYS_DEV, 128), 1)
    ray_tag = jnp.where(lane_of == SEGS_RAY, ray_of, 0)
    for k in range(SEGS_RAY):
        tags = jnp.where(lane_of == k, 1, ray_tag)
        wide[k * RAYS_DEV : (k + 1) * RAYS_DEV, in_width : in_width + 128] = tags.astype(F32).astype(
            BF16
        )
    dens_map[...] = jnp.zeros_like(dens_map)

    pick_tile = min(256, capacity)

    def tile_loop(body, size):
        for index in range(capacity // size):
            body(slice(index * size, (index + 1) * size), index)

    rows_first = (((0,), (0,)), ((), ()))

    def gather_in(step, block):
        def body(rows, index):
            first = (block * capacity + index * pick_tile).astype(F32)
            held = jnp.clip(slot_row[...] - first, -1.0, float(pick_tile)).astype(BF16)
            wanted = lax.broadcasted_iota(jnp.int32, (pick_tile, segments), 0).astype(F32).astype(BF16)
            same = jnp.broadcast_to(held, (pick_tile, segments)) == wanted
            pick = jnp.where(same, jnp.ones((), BF16), jnp.zeros((), BF16))
            mine = jnp.dot(pick, wide[...], preferred_element_type=F32)
            tag = mine[:, in_width : in_width + 128]
            turns[step, rows] = jnp.where(lane_tile < SEGS_RAY, tag, 0.0).astype(BF16)
            on_ray = lax.broadcasted_iota(jnp.int32, (pick_tile, RAYS_DEV), 1).astype(F32)
            rays[step, rows] = (tag[:, SEGS_RAY : SEGS_RAY + 1] == on_ray).astype(F32).astype(BF16)
            act[rows] = silu(
                jnp.dot(
                    mine[:, 0:in_width].astype(BF16),
                    ends[block, 0:in_width],
                    preferred_element_type=F32,
                ).astype(BF16)
            )

        tile_loop(body, pick_tile)

    lane_tile = lax.broadcasted_iota(jnp.int32, (pick_tile, 128), 1)

    def layer_step(block, layer):
        def body(rows, index):
            value = act[rows]
            act[rows] = value + silu(
                jnp.dot(value, hid[block, layer], preferred_element_type=F32).astype(BF16)
            )

        tile_loop(body, row_tile)

    def head_step(step, block):
        w_den = jnp.broadcast_to(ends[block, in_width + feats : in_width + feats + 1], (128, hidden))
        w_head = jnp.concatenate([ends[block, in_width : in_width + feats], w_den], axis=0)
        contract = (((1,), (1,)), ((), ()))

        def body(rows, index):
            out = lax.dot_general(act[rows], w_head, contract, preferred_element_type=F32)
            heads[step, rows] = out[:, 0:feats].astype(BF16)
            density = (0.25 * softplus(out[:, feats : feats + 128])).astype(BF16)
            dens_map[...] += lax.dot_general(
                turns[step, rows] * density, rays[step, rows], rows_first, preferred_element_type=F32
            )

        tile_loop(body, row_tile)

    def step_body(step, carry_in):
        block = block_at(step, place, count)
        for layer in range(layers):
            exchange(step, layer)

            @pl.when(step > 0)
            def _():
                if layer == 0:
                    move_ends(block, core_mate, 1, to_c).wait_recv()
                ready(block, layer)

            if layer == 0:
                gather_in(step, block)
            layer_step(block, layer)
        head_step(step, block)
        return carry_in

    lax.fori_loop(0, count, step_body, 0)

    density = dens_map[0:SEGS_RAY]
    optical = jnp.zeros((SEGS_RAY, RAYS_DEV), F32)
    for k in range(SEGS_RAY):
        nearer = rank_ref[k : k + 1, :] < rank_ref[...]
        optical += jnp.where(nearer, density[k : k + 1], 0.0)
    weight = jnp.exp(-optical) * (1.0 - jnp.exp(-density))
    weight = jnp.concatenate([weight, jnp.zeros((128 - SEGS_RAY, RAYS_DEV), F32)], axis=0)
    weight = weight.astype(BF16)

    def blend(step, color):
        spread = jnp.dot(turns[step], weight, preferred_element_type=F32).astype(BF16) * rays[step]
        return color + lax.dot_general(heads[step], spread, rows_first, preferred_element_type=F32)

    color = lax.fori_loop(0, count, blend, jnp.zeros((feats, RAYS_DEV), F32))
    around[4] = color.T.astype(BF16)

    def strip(dy, dx):
        edge = CONV_LAYERS * TW
        rows = {0: (0, RAYS_DEV), -1: (0, edge), 1: (RAYS_DEV - edge, edge)}[dy]
        mine = around.at[4, pl.ds(*rows)]
        theirs = around.at[(1 - dy) * 3 + 1 - dx, pl.ds(*rows)]
        return mine, theirs

    def edge_copy(index, dy, dx):
        mine, theirs = strip(dy, dx)
        there, exists = beside(dy, dx)
        return exists, pltpu.make_async_remote_copy(
            src_ref=mine,
            dst_ref=theirs,
            send_sem=edge_send.at[index],
            recv_sem=edge_recv.at[index],
            device_id=there,
            device_id_type=MESH,
        )

    for index, (dy, dx) in enumerate(AROUND):
        exists, copy = edge_copy(index, dy, dx)

        @pl.when(exists == 1)
        def _():
            copy.start()

    for index, (dy, dx) in enumerate(AROUND):
        _, arriving = edge_copy(index, dy, dx)
        _, from_there = beside(-dy, -dx)

        @pl.when(from_there == 1)
        def _():
            arriving.wait_recv()

        exists, copy = edge_copy(index, dy, dx)

        @pl.when(exists == 1)
        def _():
            copy.wait_send()

    color_ref[...] = around[...]

    own_up(lambda c: c.wait_send())
    own_down(lambda c: c.wait_send())

    def drain(step, carry_in):
        block = block_at(step, place, count)
        onward(block, lambda to: move_ends(block, core, 0, to).wait_send())
        move_ends(block, core, 1, to_c).wait_send()
        for layer in range(layers):
            onward(block, lambda to, layer=layer: move(block, layer, e_own, Z, to).wait_send())
            for kind in (X, Y, D, SA, SX, SY, SD):
                move(block, layer, e_own, kind, to_c).wait_send()
        return carry_in

    lax.fori_loop(1, count, drain, 0)


def render(count, tiles_count, rows, block_ids, ranks, w_in, w_hid, w_out, w_dens):
    segments, in_width = rows.shape
    capacity = 2 * segments // count
    layers, hidden, _ = w_hid.shape
    feats = w_out.shape[1]
    row_tile = min(512, capacity)
    end_rows = in_width + feats + 32
    vmem = pl.BlockSpec(memory_space=pltpu.VMEM)
    macs = count * capacity * hidden * (in_width + layers * hidden + feats)
    return pl.pallas_call(
        functools.partial(render_kernel, count, tiles_count, capacity, row_tile),
        out_shape=jax.ShapeDtypeStruct((9, RAYS_DEV, feats), BF16),
        in_specs=[vmem, vmem, vmem, vmem, pl.BlockSpec(memory_space=pl.ANY), vmem, vmem],
        out_specs=vmem,
        scratch_shapes=[
            pltpu.VMEM((count, layers, hidden, hidden), BF16),
            pltpu.VMEM((count, end_rows, hidden), BF16),
            pltpu.VMEM((1, segments), F32),
            pltpu.VMEM((segments, in_width + 128), BF16),
            pltpu.VMEM((count, capacity, 128), BF16),
            pltpu.VMEM((count, capacity, RAYS_DEV), BF16),
            pltpu.VMEM((capacity, hidden), BF16),
            pltpu.VMEM((count, capacity, feats), BF16),
            pltpu.VMEM((128, RAYS_DEV), F32),
            pltpu.VMEM((9, RAYS_DEV, feats), BF16),
            pltpu.SemaphoreType.DMA((8,)),
            pltpu.SemaphoreType.DMA((8,)),
            pltpu.SemaphoreType.DMA((count, layers, 9)),
            pltpu.SemaphoreType.DMA((count, layers, 8)),
            pltpu.SemaphoreType.DMA((count, 3)),
            pltpu.SemaphoreType.DMA((count, 2)),
            pltpu.SemaphoreType.DMA,
        ],
        compiler_params=pltpu.CompilerParams(
            collective_id=0, has_side_effects=True, vmem_limit_bytes=56 * 1024 * 1024
        ),
        cost_estimate=pl.CostEstimate(flops=2 * macs, bytes_accessed=4 << 20, transcendentals=0),
        name="render",
    )(rows, block_ids, ranks, w_in, w_hid, w_out, w_dens)


def conv_layer(padded, kernel, out_rows, out_cols):
    pieces = []
    for offset_y in range(3):
        for offset_x in range(3):
            pieces.append(padded[offset_y : offset_y + out_rows, offset_x : offset_x + out_cols])
    patches = jnp.concatenate(pieces, axis=-1)
    channels = kernel.shape[-1]
    result = jnp.dot(
        patches, kernel.reshape(9 * kernel.shape[2], channels), preferred_element_type=jnp.float32
    )
    center = padded[1 : 1 + out_rows, 1 : 1 + out_cols].astype(jnp.float32)
    return (center + jax.nn.silu(result)).astype(jnp.bfloat16)


def shards(seg_feat, seg_block, depth_rank, w_in, w_hidden, w_out, w_dens, conv_w):
    block_count = lax.axis_size("blocks")
    segments = seg_feat.shape[2]
    color = render(
        block_count,
        lax.axis_size("tiles"),
        seg_feat[0, 0],
        seg_block.reshape(1, segments),
        depth_rank[0, 0],
        w_in[0],
        w_hidden[0],
        w_out[0],
        w_dens,
    )
    feats = color.shape[2]
    grid = color.reshape(3, 3, TH, TW, feats)
    last = {0: slice(TH - CONV_LAYERS, TH), 1: slice(0, TH), 2: slice(0, CONV_LAYERS)}
    tile_image = jnp.concatenate(
        [
            jnp.concatenate([grid[a, b, last[a], last[b]] for b in range(3)], axis=1)
            for a in range(3)
        ],
        axis=0,
    )
    rows_total = TH * lax.axis_size(("tiles", "sub"))
    cols_total = TW * block_count
    row_pos = (
        lax.axis_index(("tiles", "sub")) * TH
        - CONV_LAYERS
        + jnp.arange(TH + 2 * CONV_LAYERS, dtype=jnp.int32)
    )
    col_pos = (
        lax.axis_index("blocks") * TW
        - CONV_LAYERS
        + jnp.arange(TW + 2 * CONV_LAYERS, dtype=jnp.int32)
    )
    inside = ((row_pos >= 0) & (row_pos < rows_total))[:, None] & (
        (col_pos >= 0) & (col_pos < cols_total)
    )[None, :]
    current = tile_image
    for layer_index in range(CONV_LAYERS):
        margin = CONV_LAYERS - layer_index - 1
        size_h = TH + 2 * margin
        size_w = TW + 2 * margin
        current = conv_layer(current, conv_w[layer_index], size_h, size_w)
        keep_mask = inside[
            layer_index + 1 : layer_index + 1 + size_h, layer_index + 1 : layer_index + 1 + size_w
        ]
        current = jnp.where(keep_mask[:, :, None], current, jnp.zeros_like(current))
    tile_image = current
    return tile_image


def solution(mesh):
    in_specs = (
        P(("groups", "tiles", "sub"), "blocks", None, None),
        P(("groups", "tiles", "sub"), "blocks", None, None),
        P(("groups", "tiles", "sub"), "blocks", None, None),
        P("blocks", None, None),
        P("blocks", None, None, None),
        P("blocks", None, None),
        P("blocks", None),
        P(),
    )
    out_specs = P(("groups", "tiles", "sub"), "blocks", None)
    return jax.shard_map(shards, mesh=mesh, in_specs=in_specs, out_specs=out_specs, check_vma=False)
```

profile of v0, /device:TPU:1, one launch (start us, length us, event | category | flops | bytes accessed | tf_op | source)
XLA Modules:
  0.0 81.6 jit_solution(9994108825069769701)
XLA Ops:
  0.0 74.3 %render.1 = bf16[9,256,128]{2,1,0:T(8,128)(2,1)} custom-call(bf16[2048,128]{1,0:T(8,128)(2,1)} %bitcast.48, s32[1,2048]{1,0:T(1,128)} %bitcast.51, s32[8,256]{1,0:T(8,128)} %bitcast.52, bf16[128,512]{1,0:T(8,128)(2,1)} %bitcast.49, bf16[4,512,512]{2,1,0:T(8,128)(2,1)} %bitcast.47, bf16[512,128]{1,0:T(8,128)(2,1)} %bitcast.50, bf16[1,512]{1,0:T(2,128)(2,1)} %w_dens_ref.1), custom_call_target="tpu_custom_call" | custom-call | flops 9663676416 | bytes 4194304 | tf_op jit(solution)/shard_map/render/pallas_call | solution.py:444
  74.3 0.8 slice_bitcast_fusion.8
  75.1 0.8 slice_bitcast_fusion.2
  75.9 0.7 slice_bitcast_fusion.4
  76.6 0.8 %slice_bitcast_fusion = bf16[16,16,128]{2,1,0:T(8,128)(2,1)S(1)} fusion(bf16[3,3,16,16,128]{4,3,2,1,0:T(8,128)(2,1)} %bitcast.46), kind=kLoop, calls=%fused_computation.33 | loop fusion | bytes 131072 | tf_op jit(solution)/shard_map/squeeze | solution.py:509
  77.4 0.1 maximum_maximum_fusion
  77.5 0.1 slice_dynamic-update-slice_fusion.6
  77.6 0.1 slice_dynamic-update-slice_fusion.5
  77.7 0.1 slice_dynamic-update-slice_fusion.16
  77.8 0.1 slice_dynamic-update-slice_fusion.3
  77.9 0.1 slice_dynamic-update-slice_fusion.1
  77.9 0.1 slice_dynamic-update-slice_fusion
  78.0 0.1 broadcast_and_fusion
  78.1 0.1 slice.173
  78.2 0.5 copy-done
  78.7 0.1 fusion.3
  78.7 0.5 fusion
  79.3 0.1 slice_dynamic-update-slice_fusion.14
  79.3 0.1 slice_dynamic-update-slice_fusion.13
  79.4 0.1 slice_dynamic-update-slice_fusion.17
  79.7 0.1 slice.172
  79.8 0.5 fusion.1
  80.6 0.1 slice.171
  80.6 1.0 %fusion.2 = bf16[16,16,128]{2,1,0:T(8,128)(2,1)} fusion(bf16[16,16,1152]{2,1,0:T(8,128)(2,1)S(1)} %slice_dynamic-update-slice_fusion.18, bf16[1152,128,1]{1,0,2:T(8,128)(2,1)S(1)} %bitcast.40, pred[16,16]{1,0:T(8,128)(4,1)S(1)} %slice.171, bf16[18,18,128]{2,1,0:T(8,128)(2,1)S(1)} %fusion.1), kind=kOutput, calls=%fused_computation.6 | convolution fusion | flops 75759616 | bytes 1016064 | tf_op jit(solution)/shard_map/dot_general | solution.py:483
  (20 shorter events, 0.6 us)
Async XLA Ops:
  77.5 1.2 %copy-start = (bf16[3,3,3,128,128]{4,3,2,1,0:T(8,128)(2,1)S(1)}, bf16[3,3,3,128,128]{4,3,2,1,0:T(8,128)(2,1)}, u32[]{:S(2)}) copy-start(bf16[3,3,3,128,128]{4,3,2,1,0:T(8,128)(2,1)} %param.15) | copy-start | bytes 2654212
where the time goes:
time: 82.2 us; the launch traced here: 81.6 us
  Pallas kernels  74.3 us (90%)
  local copies, waits for them, and re-layouts  5.02 us (6%)
  matrix products  1.97 us (2%)
    pallas_call x1, Pallas kernels, render(): pl.pallas_call(functools.partial(render_kernel, count, tiles_count, capac...  74.3 us
    squeeze x4, local copies, waits for them, and re-layouts, shards(): grid[a, b, last[a], last[b]]  3.12 us
    dot_general x3, matrix products, conv_layer(): jnp.dot(patches, kernel.reshape(9 * kernel.shape[2], channels), preferred...  1.97 us

commit v1 on v0

--- a/solution.py
+++ b/solution.py
@@ -34,6 +34,7 @@
     return jnp.where(step <= 2 * near, paired, rest)
 
 
+BUNDLE = 2
 AROUND = [(dy, dx) for dy in (-1, 0, 1) for dx in (-1, 0, 1) if (dy, dx) != (0, 0)]
 Z, X, Y, D, SA, SX, SY, SD, ZD = range(9)
 
@@ -79,6 +80,7 @@
     tx, gy = tile % 2, group % 2
     layers = w_hid_ref.shape[0]
     hidden = w_hid_ref.shape[2]
+    bundles = layers // BUNDLE
     part = hidden // 8
     end_rows = ends.shape[1]
     end_half = end_rows // 2
@@ -142,7 +144,9 @@
     pl.semaphore_wait(barrier, peers)
 
     def piece(block, layer, which):
-        return hid.at[block, layer, pl.ds(pl.multiple_of(which * part, part), part)]
+        return hid.at[
+            block, pl.ds(layer * BUNDLE, BUNDLE), pl.ds(pl.multiple_of(which * part, part), part)
+        ]
 
     def move(block, layer, which, kind, target, send_kind=None):
         ref = piece(block, layer, which)
@@ -180,14 +184,14 @@
         @pl.when(place < count - 1)
         def _():
             action(move_ends(place, core, 0, up))
-            for layer in range(layers):
+            for layer in range(bundles):
                 action(move(place, layer, e_own, Z, up))
 
     def own_down(action):
         @pl.when(place > 0)
         def _():
             action(move_ends(place, core, 0, down, 2))
-            for layer in range(layers):
+            for layer in range(bundles):
                 action(move(place, layer, e_own, Z, down, ZD))
 
     own_up(lambda c: c.start())
@@ -243,15 +247,17 @@
         return step + (layer + ahead) // layers, (layer + ahead) % layers
 
     def exchange(step, layer):
-        for ahead, action in ((4, arrive), (3, cross), (2, corner)):
+        for ahead, action in ((1, corner), (2, cross), (4, arrive)):
             later, its_layer = item(step, layer, ahead)
+            if its_layer % BUNDLE:
+                continue
 
             @pl.when((later > 0) & (later < count))
             def _():
                 block = block_at(later, place, count)
                 if action is arrive and its_layer == 0:
                     arrive_ends(block)
-                action(block, its_layer)
+                action(block, its_layer // BUNDLE)
 
     rows16 = 16
     chunks = segments // 128
@@ -348,7 +354,8 @@
             def _():
                 if layer == 0:
                     move_ends(block, core_mate, 1, to_c).wait_recv()
-                ready(block, layer)
+                if layer % BUNDLE == 0:
+                    ready(block, layer // BUNDLE)
 
             if layer == 0:
                 gather_in(step, block)
@@ -423,7 +430,7 @@
         block = block_at(step, place, count)
         onward(block, lambda to: move_ends(block, core, 0, to).wait_send())
         move_ends(block, core, 1, to_c).wait_send()
-        for layer in range(layers):
+        for layer in range(bundles):
             onward(block, lambda to, layer=layer: move(block, layer, e_own, Z, to).wait_send())
             for kind in (X, Y, D, SA, SX, SY, SD):
                 move(block, layer, e_own, kind, to_c).wait_send()
@@ -459,8 +466,8 @@
             pltpu.VMEM((9, RAYS_DEV, feats), BF16),
             pltpu.SemaphoreType.DMA((8,)),
             pltpu.SemaphoreType.DMA((8,)),
-            pltpu.SemaphoreType.DMA((count, layers, 9)),
-            pltpu.SemaphoreType.DMA((count, layers, 8)),
+            pltpu.SemaphoreType.DMA((count, layers // BUNDLE, 9)),
+            pltpu.SemaphoreType.DMA((count, layers // BUNDLE, 8)),
             pltpu.SemaphoreType.DMA((count, 3)),
             pltpu.SemaphoreType.DMA((count, 2)),
             pltpu.SemaphoreType.DMA,

time: 82.2 us -> 79.8 us (0.971)
  Pallas kernels: 74.3 us -> 71.9 us
    pallas_call x1, Pallas kernels: 74.3 us -> 71.9 us  [render(): pl.pallas_call(functools.partial(render_kernel, count, tiles_count, capac...]
where the time goes in v1:
time: 79.8 us; the launch traced here: 79.2 us
  Pallas kernels  71.9 us (90%)
  local copies, waits for them, and re-layouts  5.02 us (6%)
  matrix products  1.97 us (2%)
    pallas_call x1, Pallas kernels, render(): pl.pallas_call(functools.partial(render_kernel, count, tiles_count, capac...  71.9 us
    squeeze x4, local copies, waits for them, and re-layouts, shards(): grid[a, b, last[a], last[b]]  3.12 us
    dot_general x3, matrix products, conv_layer(): jnp.dot(patches, kernel.reshape(9 * kernel.shape[2], channels), preferred...  1.97 us

profile of v1, /device:TPU:1, one launch (start us, length us, event | category | flops | bytes accessed | tf_op | source)
XLA Modules:
  0.0 79.2 jit_solution(8895312243346956309)
XLA Ops:
  0.0 71.9 %render.1 = bf16[9,256,128]{2,1,0:T(8,128)(2,1)} custom-call(bf16[2048,128]{1,0:T(8,128)(2,1)} %bitcast.48, s32[1,2048]{1,0:T(1,128)} %bitcast.51, s32[8,256]{1,0:T(8,128)} %bitcast.52, bf16[128,512]{1,0:T(8,128)(2,1)} %bitcast.49, bf16[4,512,512]{2,1,0:T(8,128)(2,1)} %bitcast.47, bf16[512,128]{1,0:T(8,128)(2,1)} %bitcast.50, bf16[1,512]{1,0:T(2,128)(2,1)} %w_dens_ref.1), custom_call_target="tpu_custom_call" | custom-call | flops 9663676416 | bytes 4194304 | tf_op jit(solution)/shard_map/render/pallas_call | solution.py:451
  71.9 0.8 slice_bitcast_fusion.8
  72.7 0.8 slice_bitcast_fusion.2
  73.5 0.7 slice_bitcast_fusion.4
  74.2 0.8 %slice_bitcast_fusion = bf16[16,16,128]{2,1,0:T(8,128)(2,1)S(1)} fusion(bf16[3,3,16,16,128]{4,3,2,1,0:T(8,128)(2,1)} %bitcast.46), kind=kLoop, calls=%fused_computation.33 | loop fusion | bytes 131072 | tf_op jit(solution)/shard_map/squeeze | solution.py:516
  75.0 0.1 maximum_maximum_fusion
  75.1 0.1 slice_dynamic-update-slice_fusion.6
  75.2 0.1 slice_dynamic-update-slice_fusion.5
  75.3 0.1 slice_dynamic-update-slice_fusion.16
  75.4 0.1 slice_dynamic-update-slice_fusion.3
  75.5 0.1 slice_dynamic-update-slice_fusion.1
  75.5 0.1 slice_dynamic-update-slice_fusion
  75.6 0.1 broadcast_and_fusion
  75.7 0.1 slice.173
  75.7 0.5 copy-done
  76.3 0.1 fusion.3
  76.3 0.5 fusion
  76.9 0.1 slice_dynamic-update-slice_fusion.14
  76.9 0.1 slice_dynamic-update-slice_fusion.13
  77.0 0.1 slice_dynamic-update-slice_fusion.17
  77.3 0.1 slice.172
  77.3 0.5 fusion.1
  78.1 0.1 slice.171
  78.2 1.0 %fusion.2 = bf16[16,16,128]{2,1,0:T(8,128)(2,1)} fusion(bf16[16,16,1152]{2,1,0:T(8,128)(2,1)S(1)} %slice_dynamic-update-slice_fusion.18, bf16[1152,128,1]{1,0,2:T(8,128)(2,1)S(1)} %bitcast.40, pred[16,16]{1,0:T(8,128)(4,1)S(1)} %slice.171, bf16[18,18,128]{2,1,0:T(8,128)(2,1)S(1)} %fusion.1), kind=kOutput, calls=%fused_computation.6 | convolution fusion | flops 75759616 | bytes 1016064 | tf_op jit(solution)/shard_map/dot_general | solution.py:490
  (20 shorter events, 0.6 us)
Async XLA Ops:
  75.1 1.2 %copy-start = (bf16[3,3,3,128,128]{4,3,2,1,0:T(8,128)(2,1)S(1)}, bf16[3,3,3,128,128]{4,3,2,1,0:T(8,128)(2,1)}, u32[]{:S(2)}) copy-start(bf16[3,3,3,128,128]{4,3,2,1,0:T(8,128)(2,1)} %param.15) | copy-start | bytes 2654212

commit v2 on v1

--- a/solution.py
+++ b/solution.py
@@ -180,22 +180,25 @@
     m_d = eighth(1 - tx, 1 - gy, core_mate)
     up, down = {"blocks": place + 1}, {"blocks": place - 1}
 
-    def own_up(action):
-        @pl.when(place < count - 1)
-        def _():
-            action(move_ends(place, core, 0, up))
-            for layer in range(bundles):
-                action(move(place, layer, e_own, Z, up))
-
-    def own_down(action):
-        @pl.when(place > 0)
-        def _():
-            action(move_ends(place, core, 0, down, 2))
-            for layer in range(bundles):
-                action(move(place, layer, e_own, Z, down, ZD))
-
-    own_up(lambda c: c.start())
-    own_down(lambda c: c.start())
+    def own_moves(action):
+        def both(make):
+            @pl.when(place < count - 1)
+            def _():
+                action(make(up, None))
+
+            @pl.when(place > 0)
+            def _():
+                action(make(down, True))
+
+        def bundle_move(bundle):
+            both(lambda to, second: move(place, bundle, e_own, Z, to, ZD if second else None))
+
+        bundle_move(0)
+        both(lambda to, second: move_ends(place, core, 0, to, 2 if second else None))
+        for bundle in range(1, bundles):
+            bundle_move(bundle)
+
+    own_moves(lambda c: c.start())
 
     def onward(block, action):
         @pl.when((block < place) & (place < count - 1))
@@ -255,9 +258,9 @@
             @pl.when((later > 0) & (later < count))
             def _():
                 block = block_at(later, place, count)
+                action(block, its_layer // BUNDLE)
                 if action is arrive and its_layer == 0:
                     arrive_ends(block)
-                action(block, its_layer // BUNDLE)
 
     rows16 = 16
     chunks = segments // 128
@@ -421,10 +424,13 @@
         def _():
             copy.wait_send()
 
-    color_ref[...] = around[...]
-
-    own_up(lambda c: c.wait_send())
-    own_down(lambda c: c.wait_send())
+    for a in range(3):
+        for b in range(3):
+            color_ref[a * TH : (a + 1) * TH, b * TW : (b + 1) * TW] = around[a * 3 + b].reshape(
+                TH, TW, feats
+            )
+
+    own_moves(lambda c: c.wait_send())
 
     def drain(step, carry_in):
         block = block_at(step, place, count)
@@ -450,7 +456,7 @@
     macs = count * capacity * hidden * (in_width + layers * hidden + feats)
     return pl.pallas_call(
         functools.partial(render_kernel, count, tiles_count, capacity, row_tile),
-        out_shape=jax.ShapeDtypeStruct((9, RAYS_DEV, feats), BF16),
+        out_shape=jax.ShapeDtypeStruct((3 * TH, 3 * TW, feats), BF16),
         in_specs=[vmem, vmem, vmem, vmem, pl.BlockSpec(memory_space=pl.ANY), vmem, vmem],
         out_specs=vmem,
         scratch_shapes=[
@@ -508,16 +514,8 @@
         w_out[0],
         w_dens,
     )
-    feats = color.shape[2]
-    grid = color.reshape(3, 3, TH, TW, feats)
-    last = {0: slice(TH - CONV_LAYERS, TH), 1: slice(0, TH), 2: slice(0, CONV_LAYERS)}
-    tile_image = jnp.concatenate(
-        [
-            jnp.concatenate([grid[a, b, last[a], last[b]] for b in range(3)], axis=1)
-            for a in range(3)
-        ],
-        axis=0,
-    )
+    top, left = TH - CONV_LAYERS, TW - CONV_LAYERS
+    tile_image = color[top : 2 * TH + CONV_LAYERS, left : 2 * TW + CONV_LAYERS]
     rows_total = TH * lax.axis_size(("tiles", "sub"))
     cols_total = TW * block_count
     row_pos = (

time: 79.8 us -> 80.2 us (level)
  local copies, waits for them, and re-layouts: 5.02 us -> 6.18 us
    unnamed x26 -> x28, local copies, waits for them, and re-layouts: 1.47 us -> 5.75 us
    squeeze x4 -> x0, local copies, waits for them, and re-layouts: 3.12 us -> none  [shards(): grid[a, b, last[a], last[b]]]
where the time goes in v2:
time: 80.2 us; the launch traced here: 79.9 us
  Pallas kernels  71.6 us (89%)
  local copies, waits for them, and re-layouts  6.18 us (8%)
  matrix products  1.96 us (2%)
    pallas_call x1, Pallas kernels, render(): pl.pallas_call(functools.partial(render_kernel, count, tiles_count, capac...  71.6 us
    unnamed x28, local copies, waits for them, and re-layouts  5.75 us
    dot_general x3, matrix products, conv_layer(): jnp.dot(patches, kernel.reshape(9 * kernel.shape[2], channels), preferred...  1.96 us

profile of v2, /device:TPU:1, one launch (start us, length us, event | category | flops | bytes accessed | tf_op | source)
XLA Modules:
  0.0 79.9 jit_solution(3467397086559991140)
XLA Ops:
  0.0 71.6 %render.1 = bf16[48,48,128]{2,1,0:T(8,128)(2,1)} custom-call(bf16[2048,128]{1,0:T(8,128)(2,1)} %bitcast.25, s32[1,2048]{1,0:T(1,128)} %bitcast.28, s32[8,256]{1,0:T(8,128)} %bitcast.29, bf16[128,512]{1,0:T(8,128)(2,1)} %bitcast.26, bf16[4,512,512]{2,1,0:T(8,128)(2,1)} %bitcast.24, bf16[512,128]{1,0:T(8,128)(2,1)} %bitcast.27, bf16[1,512]{1,0:T(2,128)(2,1)} %w_dens_ref.1), custom_call_target="tpu_custom_call" | custom-call | flops 9663676416 | bytes 4194304 | tf_op jit(solution)/shard_map/render/pallas_call | solution.py:457
  71.6 0.0 copy-start
  71.6 0.0 copy-start.1
  71.6 1.1 %slice_dynamic-update-slice_fusion.7 = bf16[20,20,1152]{2,1,0:T(8,128)(2,1)S(1)} fusion(bf16[48,48,128]{2,1,0:T(8,128)(2,1)} %render.1), kind=kLoop, calls=%fused_computation.13 | loop fusion | bytes 225280
  72.7 1.0 %slice_dynamic-update-slice_fusion.6 = bf16[20,20,1152]{2,1,0:T(8,128)(2,1)S(1)} fusion(bf16[20,20,1152]{2,1,0:T(8,128)(2,1)S(1)} %slice_dynamic-update-slice_fusion.7, bf16[48,48,128]{2,1,0:T(8,128)(2,1)} %render.1), kind=kLoop, calls=%fused_computation.12 | loop fusion | bytes 225280
  73.7 1.0 %slice_dynamic-update-slice_fusion.5 = bf16[20,20,1152]{2,1,0:T(8,128)(2,1)S(1)} fusion(bf16[20,20,1152]{2,1,0:T(8,128)(2,1)S(1)} %slice_dynamic-update-slice_fusion.6, bf16[48,48,128]{2,1,0:T(8,128)(2,1)} %render.1), kind=kLoop, calls=%fused_computation.11 | loop fusion | bytes 225280
  74.6 1.0 %slice_dynamic-update-slice_fusion.4 = bf16[20,20,1152]{2,1,0:T(8,128)(2,1)S(1)} fusion(bf16[20,20,1152]{2,1,0:T(8,128)(2,1)S(1)} %slice_dynamic-update-slice_fusion.5, bf16[48,48,128]{2,1,0:T(8,128)(2,1)} %render.1), kind=kLoop, calls=%fused_computation.10 | loop fusion | bytes 225280
  75.6 1.0 %slice_dynamic-update-slice_fusion.16 = bf16[20,20,1152]{2,1,0:T(8,128)(2,1)S(1)} fusion(bf16[20,20,1152]{2,1,0:T(8,128)(2,1)S(1)} %slice_dynamic-update-slice_fusion.4, bf16[48,48,128]{2,1,0:T(8,128)(2,1)} %render.1), kind=kLoop, calls=%fused_computation.22 | loop fusion | bytes 225280
  76.6 0.1 slice_dynamic-update-slice_fusion.3
  76.7 0.1 slice_dynamic-update-slice_fusion.2
  76.7 0.1 slice_dynamic-update-slice_fusion.1
  76.8 0.1 slice_dynamic-update-slice_fusion
  76.9 0.1 broadcast_and_fusion
  76.9 0.1 slice.147
  77.0 0.1 fusion.3
  77.1 0.5 fusion
  77.6 0.1 slice_dynamic-update-slice_fusion.14
  77.7 0.1 slice_dynamic-update-slice_fusion.13
  77.8 0.1 slice_dynamic-update-slice_fusion.17
  77.8 0.1 slice_dynamic-update-slice_fusion.11
  78.0 0.1 slice.146
  78.1 0.5 fusion.1
  78.9 0.1 slice.145
  79.0 1.0 %fusion.2 = bf16[16,16,128]{2,1,0:T(8,128)(2,1)} fusion(bf16[16,16,1152]{2,1,0:T(8,128)(2,1)S(1)} %slice_dynamic-update-slice_fusion.18, bf16[1152,128,1]{1,0,2:T(8,128)(2,1)S(1)} %bitcast.21, pred[16,16]{1,0:T(8,128)(4,1)S(1)} %slice.145, bf16[18,18,128]{2,1,0:T(8,128)(2,1)S(1)} %fusion.1), kind=kOutput, calls=%fused_computation.5 | convolution fusion | flops 75759616 | bytes 1016064 | tf_op jit(solution)/shard_map/dot_general | solution.py:496
  (17 shorter events, 0.5 us)
Async XLA Ops:
  71.6 5.0 %copy-start = (bf16[48,48,128]{2,1,0:T(8,128)(2,1)S(1)}, bf16[48,48,128]{2,1,0:T(8,128)(2,1)}, u32[]{:S(2)}) copy-start(bf16[48,48,128]{2,1,0:T(8,128)(2,1)} %render.1) | copy-start | bytes 1769476
  71.6 5.4 %copy-start.1 = (bf16[3,3,3,128,128]{4,3,2,1,0:T(8,128)(2,1)S(1)}, bf16[3,3,3,128,128]{4,3,2,1,0:T(8,128)(2,1)}, u32[]{:S(2)}) copy-start(bf16[3,3,3,128,128]{4,3,2,1,0:T(8,128)(2,1)} %param.15) | copy-start | bytes 2654212

commit v3 on v2

--- a/solution.py
+++ b/solution.py
@@ -515,7 +515,9 @@
         w_dens,
     )
     top, left = TH - CONV_LAYERS, TW - CONV_LAYERS
-    tile_image = color[top : 2 * TH + CONV_LAYERS, left : 2 * TW + CONV_LAYERS]
+    tile_image = lax.optimization_barrier(
+        color[top : 2 * TH + CONV_LAYERS, left : 2 * TW + CONV_LAYERS]
+    )
     rows_total = TH * lax.axis_size(("tiles", "sub"))
     cols_total = TW * block_count
     row_pos = (

time: 80.2 us -> 76.9 us (0.959)
  local copies, waits for them, and re-layouts: 6.18 us -> 2.87 us
    unnamed x28 -> x26, local copies, waits for them, and re-layouts: 5.75 us -> 1.47 us
    slice x0 -> x1, local copies, waits for them, and re-layouts: none -> 0.97 us  [shards(): color[top:2 * TH + CONV_LAYERS, left:2 * TW + CONV_LAYERS]]
where the time goes in v3:
time: 76.9 us; the launch traced here: 76.6 us
  Pallas kernels  71.6 us (93%)
  local copies, waits for them, and re-layouts  2.87 us (4%)
  matrix products  1.97 us (3%)
    pallas_call x1, Pallas kernels, render(): pl.pallas_call(functools.partial(render_kernel, count, tiles_count, capac...  71.6 us
    dot_general x3, matrix products, conv_layer(): jnp.dot(patches, kernel.reshape(9 * kernel.shape[2], channels), preferred...  1.97 us

profile of v3, /device:TPU:1, one launch (start us, length us, event | category | flops | bytes accessed | tf_op | source)
XLA Modules:
  0.0 76.6 jit_solution(16047081876035646782)
XLA Ops:
  0.0 71.6 %render.1 = bf16[48,48,128]{2,1,0:T(8,128)(2,1)} custom-call(bf16[2048,128]{1,0:T(8,128)(2,1)} %bitcast.25, s32[1,2048]{1,0:T(1,128)} %bitcast.28, s32[8,256]{1,0:T(8,128)} %bitcast.29, bf16[128,512]{1,0:T(8,128)(2,1)} %bitcast.26, bf16[4,512,512]{2,1,0:T(8,128)(2,1)} %bitcast.24, bf16[512,128]{1,0:T(8,128)(2,1)} %bitcast.27, bf16[1,512]{1,0:T(2,128)(2,1)} %w_dens_ref.1), custom_call_target="tpu_custom_call" | custom-call | flops 9663676416 | bytes 4194304 | tf_op jit(solution)/shard_map/render/pallas_call | solution.py:457
  71.6 1.0 %slice.108 = bf16[22,22,128]{2,1,0:T(8,128)(2,1)S(1)} slice(bf16[48,48,128]{2,1,0:T(8,128)(2,1)} %render.1), slice={[13:35], [13:35], [0:128]} | slice | bytes 247808 | tf_op jit(solution)/shard_map/slice | solution.py:519
  72.5 0.0 copy-start
  72.6 0.1 slice_dynamic-update-slice_fusion.6
  72.6 0.1 slice_dynamic-update-slice_fusion.5
  72.7 0.1 slice_dynamic-update-slice_fusion.16
  72.8 0.1 slice_dynamic-update-slice_fusion.3
  72.9 0.1 slice_dynamic-update-slice_fusion.1
  73.0 0.1 slice_dynamic-update-slice_fusion
  73.0 0.1 broadcast_and_fusion
  73.1 0.1 slice.141
  73.2 0.5 copy-done
  73.7 0.1 fusion.3
  73.8 0.5 fusion
  74.3 0.1 slice_dynamic-update-slice_fusion.14
  74.4 0.1 slice_dynamic-update-slice_fusion.13
  74.5 0.1 slice_dynamic-update-slice_fusion.17
  74.5 0.1 slice_dynamic-update-slice_fusion.11
  74.7 0.1 slice.140
  74.8 0.5 fusion.1
  75.6 0.1 slice.139
  75.7 1.0 %fusion.2 = bf16[16,16,128]{2,1,0:T(8,128)(2,1)} fusion(bf16[16,16,1152]{2,1,0:T(8,128)(2,1)S(1)} %slice_dynamic-update-slice_fusion.18, bf16[1152,128,1]{1,0,2:T(8,128)(2,1)S(1)} %bitcast.21, pred[16,16]{1,0:T(8,128)(4,1)S(1)} %slice.139, bf16[18,18,128]{2,1,0:T(8,128)(2,1)S(1)} %fusion.1), kind=kOutput, calls=%fused_computation.5 | convolution fusion | flops 75759616 | bytes 1016064 | tf_op jit(solution)/shard_map/dot_general | solution.py:496
  (18 shorter events, 0.6 us)
Async XLA Ops:
  72.5 1.2 %copy-start = (bf16[3,3,3,128,128]{4,3,2,1,0:T(8,128)(2,1)S(1)}, bf16[3,3,3,128,128]{4,3,2,1,0:T(8,128)(2,1)}, u32[]{:S(2)}) copy-start(bf16[3,3,3,128,128]{4,3,2,1,0:T(8,128)(2,1)} %param.15) | copy-start | bytes 2654212

commit v4 on v3

--- a/solution.py
+++ b/solution.py
@@ -250,7 +250,7 @@
         return step + (layer + ahead) // layers, (layer + ahead) % layers
 
     def exchange(step, layer):
-        for ahead, action in ((1, corner), (2, cross), (4, arrive)):
+        for ahead, action in ((3, corner), (4, cross), (6, arrive)):
             later, its_layer = item(step, layer, ahead)
             if its_layer % BUNDLE:
                 continue
@@ -366,6 +366,9 @@
         head_step(step, block)
         return carry_in
 
+    next_block = block_at(1, place, count)
+    arrive(next_block, 0)
+    arrive_ends(next_block)
     lax.fori_loop(0, count, step_body, 0)
 
     density = dens_map[0:SEGS_RAY]

time: 76.9 us -> 77.4 us (level)
  no operation moved by 1% of the time
where the time goes in v4:
time: 77.4 us; the launch traced here: 76.7 us
  Pallas kernels  71.6 us (93%)
  local copies, waits for them, and re-layouts  2.87 us (4%)
  matrix products  1.96 us (3%)
    pallas_call x1, Pallas kernels, render(): pl.pallas_call(functools.partial(render_kernel, count, tiles_count, capac...  71.6 us
    dot_general x3, matrix products, conv_layer(): jnp.dot(patches, kernel.reshape(9 * kernel.shape[2], channels), preferred...  1.96 us

profile of v4, /device:TPU:1, one launch (start us, length us, event | category | flops | bytes accessed | tf_op | source)
XLA Modules:
  0.0 76.7 jit_solution(5550069220625685643)
XLA Ops:
  0.0 71.6 %render.1 = bf16[48,48,128]{2,1,0:T(8,128)(2,1)} custom-call(bf16[2048,128]{1,0:T(8,128)(2,1)} %bitcast.25, s32[1,2048]{1,0:T(1,128)} %bitcast.28, s32[8,256]{1,0:T(8,128)} %bitcast.29, bf16[128,512]{1,0:T(8,128)(2,1)} %bitcast.26, bf16[4,512,512]{2,1,0:T(8,128)(2,1)} %bitcast.24, bf16[512,128]{1,0:T(8,128)(2,1)} %bitcast.27, bf16[1,512]{1,0:T(2,128)(2,1)} %w_dens_ref.1), custom_call_target="tpu_custom_call" | custom-call | flops 9663676416 | bytes 4194304 | tf_op jit(solution)/shard_map/render/pallas_call | solution.py:460
  71.6 1.0 %slice.108 = bf16[22,22,128]{2,1,0:T(8,128)(2,1)S(1)} slice(bf16[48,48,128]{2,1,0:T(8,128)(2,1)} %render.1), slice={[13:35], [13:35], [0:128]} | slice | bytes 247808 | tf_op jit(solution)/shard_map/slice | solution.py:522
  72.6 0.0 copy-start
  72.6 0.1 slice_dynamic-update-slice_fusion.6
  72.7 0.1 slice_dynamic-update-slice_fusion.5
  72.8 0.1 slice_dynamic-update-slice_fusion.16
  72.9 0.1 slice_dynamic-update-slice_fusion.3
  73.0 0.1 slice_dynamic-update-slice_fusion.1
  73.0 0.1 slice_dynamic-update-slice_fusion
  73.1 0.1 broadcast_and_fusion
  73.2 0.1 slice.141
  73.3 0.5 copy-done
  73.8 0.1 fusion.3
  73.8 0.5 fusion
  74.4 0.1 slice_dynamic-update-slice_fusion.14
  74.4 0.1 slice_dynamic-update-slice_fusion.13
  74.5 0.1 slice_dynamic-update-slice_fusion.17
  74.6 0.1 slice_dynamic-update-slice_fusion.11
  74.8 0.1 slice.140
  74.8 0.5 fusion.1
  75.6 0.1 slice.139
  75.7 1.0 %fusion.2 = bf16[16,16,128]{2,1,0:T(8,128)(2,1)} fusion(bf16[16,16,1152]{2,1,0:T(8,128)(2,1)S(1)} %slice_dynamic-update-slice_fusion.18, bf16[1152,128,1]{1,0,2:T(8,128)(2,1)S(1)} %bitcast.21, pred[16,16]{1,0:T(8,128)(4,1)S(1)} %slice.139, bf16[18,18,128]{2,1,0:T(8,128)(2,1)S(1)} %fusion.1), kind=kOutput, calls=%fused_computation.5 | convolution fusion | flops 75759616 | bytes 1016064 | tf_op jit(solution)/shard_map/dot_general | solution.py:499
  (18 shorter events, 0.6 us)
Async XLA Ops:
  72.6 1.2 %copy-start = (bf16[3,3,3,128,128]{4,3,2,1,0:T(8,128)(2,1)S(1)}, bf16[3,3,3,128,128]{4,3,2,1,0:T(8,128)(2,1)}, u32[]{:S(2)}) copy-start(bf16[3,3,3,128,128]{4,3,2,1,0:T(8,128)(2,1)} %param.15) | copy-start | bytes 2654212
